TPU v7x, 32 devices: a whole 2x2x4 slice. The times are simulated.
32 devices in a mesh: passage: 4 (over z), span: 8 (over y, x, core).
Axes of the slice: x: 2, y: 2, z: 4, core: 2. Of those that a mesh axis runs over, the one named last changes fastest.
Arguments:
- psi_rotor: float32 [6, 64, 64, 128], P(None, 'passage', 'span'), may hold values from -11 to 11
- psi_stator: float32 [6, 64, 64, 128], P(None, 'passage', 'span'), may hold values from -6 to 6
- rhs_rotor: float32 [6, 64, 64, 128], P(None, 'passage', 'span'), may hold values from -6 to 6
- rhs_stator: float32 [6, 64, 64, 128], P(None, 'passage', 'span'), may hold values from -6 to 6
- kappa_rotor: float32 [64, 64, 128], P('passage', 'span'), may hold values from 1 to 4
- kappa_stator: float32 [64, 64, 128], P('passage', 'span'), may hold values from 1 to 4
- rotor_blocks: float32 [7, 6, 6], replicated, may hold values from -0.5 to 1
- stator_blocks: float32 [7, 6, 6], replicated, may hold values from -0.5 to 1
- interface_block: float32 [6, 6], replicated, may hold values from -0.5 to 0.7
- pass_counts: int32 [4], P('passage'), may hold values from 8 to 16
- tile_source: int32 [8], replicated, may hold values from 0 to 7, as said below
Outputs:
- rotor_out: float32 [6, 64, 64, 128], P(None, 'passage', 'span')
- stator_out: float32 [6, 64, 64, 128], P(None, 'passage', 'span')
Inputs may be any that keep to these rules, and one draw needn't show every extreme that they name: `tile_source`: each stator span tile names one rotor span tile.
All inputs are finite; a program needn't handle non-finite values.
Results may differ from a plain program's by a relative error of at most 0.00011.
Values sent between devices are 32-bit elements; how exact they have to be, the bound alone decides.
A program may use at most 64 MiB of HBM per device.

v0:
```python
import functools

import jax
import jax.numpy as jnp
from jax import lax
from jax.experimental import pallas as pl
from jax.experimental.pallas import tpu as pltpu
from jax.sharding import PartitionSpec as P

ITERS = 3
RELAX = 0.8
MESH = pl.DeviceIdType.MESH
F32 = jnp.float32
BF16 = jnp.bfloat16
ROTOR, STATOR = 0, 1


def split(x):
    hi = x.astype(BF16)
    lo = (x - hi.astype(F32)).astype(BF16)
    return hi, lo


def kernel(fields, cp, cs, ca, npass, nspan, *refs):
    it = iter(refs)

    def take(n):
        return [next(it) for _ in range(n)]

    psi_in = take(2)
    rhs_in = take(2)
    kap_in = take(2)
    blocks = take(2)
    (iface, counts, source) = take(3)
    outs = take(2)
    psi = [take(ITERS + 1) for _ in range(2)]
    rhs = take(2)
    coef = take(2)
    cen = [[take(2) for _ in range(ITERS)] for _ in range(2)]
    ext = [[take(2) for _ in range(ITERS)] for _ in range(2)]
    mat = take(2)
    (psend, precv, ssend, srecv, fsend, frecv, msend) = take(7)
    mrecv = take(ITERS)
    (in_sem, out_sem, hs_sem, hr_sem, fs_sem, fr_sem, ms_sem, mr_sem) = take(8)

    nb = fields * cs
    kx = 2 * nb + 16
    plane = cp * cs

    ip = lax.axis_index("passage")
    js = lax.axis_index("span")
    right = lax.rem(ip + 1, npass)
    left = lax.rem(ip + npass - 1, npass)

    srecv[...] = jnp.zeros_like(srecv)

    barrier = pltpu.get_barrier_semaphore()
    for o in range(1, npass):
        pl.semaphore_signal(
            barrier, inc=1, device_id=(lax.rem(ip + o, npass), js), device_id_type=MESH
        )
    for o in range(1, nspan):
        pl.semaphore_signal(
            barrier, inc=1, device_id=(ip, lax.rem(js + o, nspan)), device_id_type=MESH
        )

    loads = {}
    for n, (src, dst, name) in enumerate(
        [
            (psi_in[0], psi[0][0], "psi0"),
            (psi_in[1], psi[1][0], "psi1"),
            (kap_in[0], coef[0], "kap0"),
            (rhs_in[0], rhs[0], "rhs0"),
            (kap_in[1], coef[1], "kap1"),
            (rhs_in[1], rhs[1], "rhs1"),
        ]
    ):
        loads[name] = pltpu.make_async_copy(src, dst, in_sem.at[n])
        loads[name].start()

    def halo_copies(r, k):
        made = []
        for d, target in ((0, (right, js)), (1, (left, js))):
            made.append(
                pltpu.make_async_remote_copy(
                    src_ref=psend.at[r, k, d],
                    dst_ref=precv.at[r, k, d],
                    send_sem=hs_sem.at[r, k, d],
                    recv_sem=hr_sem.at[r, k, d],
                    device_id=target,
                    device_id_type=MESH,
                )
            )
        for d, target in (
            (0, (ip, lax.rem(js + 1, nspan))),
            (1, (ip, lax.rem(js + nspan - 1, nspan))),
        ):
            made.append(
                pltpu.make_async_remote_copy(
                    src_ref=ssend.at[r, k, d],
                    dst_ref=srecv.at[r, k, d, pl.ds(0, fields * cp)],
                    send_sem=hs_sem.at[r, k, 2 + d],
                    recv_sem=hr_sem.at[r, k, 2 + d],
                    device_id=target,
                    device_id_type=MESH,
                )
            )
        return made

    halos = {(r, k): halo_copies(r, k) for r in range(2) for k in range(ITERS)}
    has_next, has_prev = js < nspan - 1, js > 0

    def pack_halos(r, k):
        for d, p in ((0, cp - 1), (1, 0)):
            for f in range(fields):
                psend[r, k, d, pl.ds(f * cs, cs), :] = psi[r][k][
                    pl.ds(f * plane + p * cs, cs), :
                ]
        for d, s in ((0, cs - 1), (1, 0)):
            for f in range(fields):
                ssend[r, k, d, pl.ds(f * cp, cp), :] = psi[r][k][
                    pl.ds(f * plane + s, cp, stride=cs), :
                ]

    def start_halos(r, k):
        to_right, to_left, to_next, to_prev = halos[r, k]

        @pl.when(has_next)
        def _():
            to_next.start()

        @pl.when(has_prev)
        def _():
            to_prev.start()

        to_right.start()
        to_left.start()

    def finish_sends(r, k):
        to_right, to_left, to_next, to_prev = halos[r, k]
        to_right.wait_send()
        to_left.wait_send()

        @pl.when(has_next)
        def _():
            to_next.wait_send()

        @pl.when(has_prev)
        def _():
            to_prev.wait_send()

    def receive_halos(r, k):
        to_right, to_left, to_next, to_prev = halos[r, k]
        to_right.wait_recv()
        to_left.wait_recv()

        @pl.when(has_prev)
        def _():
            to_next.wait_recv()

        @pl.when(has_next)
        def _():
            to_prev.wait_recv()

        chi, clo = cen[r][k]
        for d, p in ((0, 0), (1, cp + 1)):
            hi, lo = split(precv[r, k, d])
            chi[pl.ds(p * nb, nb), :] = hi
            clo[pl.ds(p * nb, nb), :] = lo
        xhi, xlo = ext[r][k]
        for p in range(cp):
            rows = [srecv[r, k, d, pl.ds(p, 8, stride=cp), :] for d in range(2)]
            hi, lo = split(jnp.concatenate(rows, axis=0))
            xhi[pl.ds(p * kx + 2 * nb, 16), :] = hi
            xlo[pl.ds(p * kx + 2 * nb, 16), :] = lo

    lane = lax.broadcasted_iota(jnp.int32, (cs, ca), 1)
    wide = lax.broadcasted_iota(jnp.int32, (nb, ca), 1)

    def face_copies(k):
        return [
            pltpu.make_async_remote_copy(
                src_ref=fsend.at[k],
                dst_ref=frecv.at[k, o],
                send_sem=fs_sem.at[k, o],
                recv_sem=fr_sem.at[k, o],
                device_id=(lax.rem(ip + o, npass), js),
                device_id_type=MESH,
            )
            for o in range(1, npass)
        ]

    def mean_copies(k):
        return [
            pltpu.make_async_remote_copy(
                src_ref=msend.at[k],
                dst_ref=mrecv[k].at[js],
                send_sem=ms_sem.at[k, o],
                recv_sem=mr_sem.at[k, o],
                device_id=(ip, lax.rem(js + o, nspan)),
                device_id_type=MESH,
            )
            for o in range(1, nspan)
        ]

    faces = [face_copies(k) for k in range(ITERS)]
    means = [mean_copies(k) for k in range(ITERS)]
    count = counts[0]

    def pack_face(k):
        state = psi[ROTOR][k]
        tile = jnp.where(lane == fields, jnp.clip(count, 0, cp).astype(F32), 0.0)
        for f in range(fields):
            acc = jnp.zeros((cs, ca), F32)
            for p in range(cp):
                w = jnp.where(p < count, 1.0, 0.0).astype(F32)
                acc = acc + w * state[pl.ds(f * plane + p * cs, cs), :]
            tile = jnp.where(lane == f, pltpu.roll(acc, f + 1, 1), tile)
        fsend[k] = tile

    def start_face(k):
        for c in faces[k]:
            c.start()

    def send_mean(k):
        total = fsend[k]
        for o, c in enumerate(faces[k]):
            c.wait_recv()
            total = total + frecv[k, o + 1]
        mean = total / total[:, fields : fields + 1]
        msend[k] = mean
        mrecv[k][js] = mean
        for c in means[k]:
            c.start()

    def inlet_rows(k):
        for c in means[k]:
            c.wait_recv()
        tile = mrecv[k][source[js]]
        moved = [
            jnp.where(lane == 0, pltpu.roll(tile, (ca - g) % ca, 1), 0.0) for g in range(fields)
        ]
        rows = []
        for f in range(fields):
            acc = iface[f, 0] * moved[0]
            for g in range(1, fields):
                acc = acc + iface[f, g] * moved[g]
            rows.append(acc)
        return jnp.concatenate(rows, axis=0)

    def build_matrix(r):
        kk = 5 * nb + 16
        col = lax.broadcasted_iota(jnp.int32, (cs, kk), 1)
        row = lax.broadcasted_iota(jnp.int32, (cs, kk), 0)
        part = col // nb
        g_in = (col - part * nb) // cs
        s_in = col - part * nb - g_in * cs
        tail = part == 5
        up = tail & (g_in == 0)
        down = tail & (g_in == 1)
        which = jnp.full((cs, kk), -1, jnp.int32)
        same = s_in == row
        which = jnp.where((part == 0) & same, 1, which)
        which = jnp.where((part == 2) & same, 2, which)
        which = jnp.where((part == 3) & same, 5, which)
        which = jnp.where((part == 4) & same, 6, which)
        which = jnp.where((part == 1) & (s_in + 1 == row), 3, which)
        which = jnp.where((part == 1) & (s_in == row + 1), 4, which)
        which = jnp.where(up & (row == 0), 3, which)
        which = jnp.where(down & (row == cs - 1), 4, which)
        field = jnp.where(tail, s_in, g_in)
        code = jnp.where(which >= 0, which * 8 + field, -1)
        middle = jnp.where((part == 1) & same, g_in, -1)
        near, main = [], []
        masks = [[code == (b * 8 + g) for g in range(fields)] for b in range(1, 7)]
        centre = [middle == g for g in range(fields)]
        for f in range(fields):
            acc = jnp.zeros((cs, kk), F32)
            mid = jnp.zeros((cs, kk), F32)
            for g in range(fields):
                mid = jnp.where(centre[g], -RELAX * blocks[r][f, 0, g], mid)
                for b in range(1, 7):
                    acc = jnp.where(masks[b - 1][g], blocks[r][f, b, g], acc)
            near.append(acc)
            main.append(mid)
        hi, lo = split(jnp.concatenate(near + main, axis=0))
        mat[r][pl.ds(0, 2 * nb), :] = hi
        mat[r][pl.ds(2 * nb, 2 * nb), :] = lo

    def store_split(r, k, p, new):
        chi, clo = cen[r][k]
        xhi, xlo = ext[r][k]
        hi, lo = split(new)
        at = pl.ds(pl.multiple_of((p + 1) * nb, 16), nb)
        chi[at, :] = hi
        clo[at, :] = lo
        before = jnp.where(wide == 0, 0.0, pltpu.roll(new, 1, 1))
        after = jnp.where(wide == ca - 1, 0.0, pltpu.roll(new, ca - 1, 1))
        for n, value in enumerate((before, after)):
            hi, lo = split(value)
            at = pl.ds(pl.multiple_of(p * kx + n * nb, 16), nb)
            xhi[at, :] = hi
            xlo[at, :] = lo

    def cell(ref, p):
        return jnp.concatenate(
            [ref[pl.ds(pl.multiple_of(f * plane + p * cs, 8), cs), :] for f in range(fields)],
            axis=0,
        )

    def columns(c, x, p):
        return jnp.concatenate(
            [
                c[pl.ds(pl.multiple_of(p * nb, 16), 3 * nb), :],
                x[pl.ds(pl.multiple_of(p * kx, 16), kx), :],
            ],
            axis=0,
        )

    def advance(r, k, inlet):
        chi, clo = cen[r][k]
        xhi, xlo = ext[r][k]

        def pair(q):
            cells = (2 * q, 2 * q + 1)
            hi = jnp.concatenate([columns(chi, xhi, p) for p in cells], axis=1)
            lo = jnp.concatenate([columns(clo, xlo, p) for p in cells], axis=1)
            first = jnp.dot(mat[r][...], hi, preferred_element_type=F32)
            second = jnp.dot(mat[r][pl.ds(0, 2 * nb), :], lo, preferred_element_type=F32)
            both = first[: 2 * nb] + (first[2 * nb :] + second)
            for n, p in enumerate(cells):
                mine = both[:, n * ca : (n + 1) * ca]
                res = cell(rhs[r], p) + mine[:nb]
                if inlet is not None:
                    res = res + inlet
                c = coef[r][pl.ds(pl.multiple_of(p * cs, 8), cs), :]
                c = jnp.concatenate([c] * fields, axis=0)
                new = (cell(psi[r][k], p) + mine[nb:]) + c * res
                for f in range(fields):
                    psi[r][k + 1][pl.ds(pl.multiple_of(f * plane + p * cs, 8), cs), :] = new[
                        f * cs : (f + 1) * cs
                    ]
                if k + 1 < ITERS:
                    store_split(r, k + 1, p, new)

        pl.loop(0, cp // 2, unroll=cp // 2)(pair)

    for r in range(2):
        build_matrix(r)
    for r in range(2):
        loads["psi%d" % r].wait()
        pl.loop(0, cp, unroll=cp)(lambda p, r=r: store_split(r, 0, p, cell(psi[r][0], p)))
        pack_halos(r, 0)
    pack_face(0)
    for r in range(2):
        loads["kap%d" % r].wait()
        coef[r][...] = RELAX / coef[r][...]
        loads["rhs%d" % r].wait()

    pl.semaphore_wait(barrier, npass + nspan - 2)
    start_face(0)
    start_halos(ROTOR, 0)
    start_halos(STATOR, 0)

    stores = []
    for k in range(ITERS):
        send_mean(k)
        receive_halos(ROTOR, k)
        advance(ROTOR, k, None)
        if k + 1 < ITERS:
            pack_face(k + 1)
            start_face(k + 1)
            pack_halos(ROTOR, k + 1)
            start_halos(ROTOR, k + 1)
        else:
            stores.append(pltpu.make_async_copy(psi[ROTOR][ITERS], outs[ROTOR], out_sem.at[0]))
            stores[-1].start()
        inlet = inlet_rows(k)
        receive_halos(STATOR, k)
        advance(STATOR, k, inlet)
        if k + 1 < ITERS:
            pack_halos(STATOR, k + 1)
            start_halos(STATOR, k + 1)
    stores.append(pltpu.make_async_copy(psi[STATOR][ITERS], outs[STATOR], out_sem.at[1]))
    stores[-1].start()
    for k in range(ITERS):
        for r in range(2):
            finish_sends(r, k)
        for c in faces[k] + means[k]:
            c.wait_send()
    for c in stores:
        c.wait()


def per_device(
    npass,
    nspan,
    psi_rotor,
    psi_stator,
    rhs_rotor,
    rhs_stator,
    kappa_rotor,
    kappa_stator,
    rotor_blocks,
    stator_blocks,
    interface_block,
    pass_counts,
    tile_source,
):
    fields, cp, cs, ca = psi_rotor.shape
    rows = fields * cp * cs
    flat = [x.reshape(rows, ca) for x in (psi_rotor, psi_stator, rhs_rotor, rhs_stator)]
    kaps = [x.reshape(cp * cs, ca) for x in (kappa_rotor, kappa_stator)]
    nb = fields * cs
    kx = 2 * nb + 16
    state = pltpu.VMEM((rows, ca), F32)
    scratch = [state] * (2 * (ITERS + 1))
    scratch += [state] * 2
    scratch += [pltpu.VMEM((cp * cs, ca), F32)] * 2
    scratch += [pltpu.VMEM(((cp + 2) * nb, ca), BF16)] * (2 * ITERS * 2)
    scratch += [pltpu.VMEM((cp * kx, ca), BF16)] * (2 * ITERS * 2)
    scratch += [pltpu.VMEM((4 * nb, 5 * nb + 16), BF16)] * 2
    scratch += [
        pltpu.VMEM((2, ITERS, 2, nb, ca), F32),
        pltpu.VMEM((2, ITERS, 2, nb, ca), F32),
        pltpu.VMEM((2, ITERS, 2, fields * cp, ca), F32),
        pltpu.VMEM((2, ITERS, 2, 8 * cp, ca), F32),
        pltpu.VMEM((ITERS, cs, ca), F32),
        pltpu.VMEM((ITERS, npass, cs, ca), F32),
        pltpu.VMEM((ITERS, cs, ca), F32),
    ]
    scratch += [pltpu.VMEM((nspan, cs, ca), F32)] * ITERS
    dma = pltpu.SemaphoreType.DMA
    scratch += [
        dma((6,)),
        dma((2,)),
        dma((2, ITERS, 4)),
        dma((2, ITERS, 4)),
        dma((ITERS, npass)),
        dma((ITERS, npass)),
        dma((ITERS, nspan)),
        dma((ITERS, nspan)),
    ]
    anywhere = pl.BlockSpec(memory_space=pltpu.HBM)
    smem = pl.BlockSpec(memory_space=pltpu.SMEM)
    out = pl.pallas_call(
        functools.partial(kernel, fields, cp, cs, ca, npass, nspan),
        out_shape=[pltpu.HBM((rows, ca), F32)] * 2,
        in_specs=[anywhere] * 6 + [smem] * 5,
        out_specs=[anywhere] * 2,
        scratch_shapes=scratch,
        compiler_params=pltpu.CompilerParams(
            collective_id=0, has_side_effects=True, vmem_limit_bytes=40 * 1024 * 1024
        ),
    )(
        *[pltpu.with_memory_space_constraint(x, pltpu.HBM) for x in flat + kaps],
        rotor_blocks.transpose(1, 0, 2),
        stator_blocks.transpose(1, 0, 2),
        interface_block,
        pass_counts,
        tile_source,
    )
    return tuple(x.reshape(psi_rotor.shape) for x in out)


def solution(mesh):
    return jax.shard_map(
        functools.partial(per_device, mesh.shape["passage"], mesh.shape["span"]),
        mesh=mesh,
        in_specs=(
            P(None, "passage", "span", None),
            P(None, "passage", "span", None),
            P(None, "passage", "span", None),
            P(None, "passage", "span", None),
            P("passage", "span", None),
            P("passage", "span", None),
            P(),
            P(),
            P(),
            P("passage"),
            P(),
        ),
        out_specs=(P(None, "passage", "span", None), P(None, "passage", "span", None)),
        check_vma=False,
    )
```

profile of v0, /device:TPU:0, one launch (start us, length us, event | category | flops | bytes accessed | tf_op | source)
XLA Modules:
  0.0 32.1 jit_solution(10441656070957988915)
XLA Ops:
  1.3 0.0 copy-start.2
  1.3 0.0 copy-start.3
  1.3 0.7 %copy-done.2 = f32[6,6]{1,0:T(8,128)S(1)} copy-done((f32[6,6]{1,0:T(8,128)S(1)}, f32[6,6]{1,0:T(8,128)}, u32[]{:S(2)}) %copy-start.2) | copy-done | bytes 168
  2.0 0.0 copy-done.3
  2.0 0.0 copy-start
  2.0 0.7 %copy-done = f32[7,6,6]{2,0,1:T(8,128)S(1)} copy-done((f32[7,6,6]{2,0,1:T(8,128)S(1)}, f32[7,6,6]{2,0,1:T(8,128)}, u32[]{:S(2)}) %copy-start) | copy-done | bytes 1032
  2.7 0.0 copy-start.1
  2.7 0.7 %copy-done.1 = f32[7,6,6]{2,0,1:T(8,128)S(1)} copy-done((f32[7,6,6]{2,0,1:T(8,128)S(1)}, f32[7,6,6]{2,0,1:T(8,128)}, u32[]{:S(2)}) %copy-start.1) | copy-done | bytes 1032
  3.4 26.1 %shard_map.122 = (f32[768,128]{1,0:T(8,128)}, f32[768,128]{1,0:T(8,128)}) custom-call(f32[768,128]{1,0:T(8,128)} %bitcast.14, f32[768,128]{1,0:T(8,128)} %bitcast.15, f32[768,128]{1,0:T(8,128)} %bitcast.16, f32[768,128]{1,0:T(8,128)} %bitcast.17, f32[128,128]{1,0:T(8,128)} %bitcast.18, f32[128,128]{1,0:T(8,128)} %bitcast.19, f32[6,7,6]{2,1,0:T(8,128)S(1)} %bitcast.10, ...), custom_call_target="tpu_custom_call" | custom-call | tf_op jit(solution)/shard_map/pallas_call | solution.py:446
  29.5 0.0 copy-start.4
  29.5 1.8 %copy.16 = f32[6,16,8,128]{3,2,1,0:T(8,128)} copy(f32[6,16,8,128]{3,2,1,0:T(8,128)} %bitcast.13) | data formatting | bytes 786432
  31.4 0.0 copy-done.4
  31.4 0.7 %copy.17 = f32[6,16,8,128]{3,2,1,0:T(8,128)} copy(f32[6,16,8,128]{3,2,1,0:T(8,128)S(1)} %bitcast.12) | data formatting | bytes 786432
Async XLA Ops:
  1.3 0.7 %copy-start.2 = (f32[6,6]{1,0:T(8,128)S(1)}, f32[6,6]{1,0:T(8,128)}, u32[]{:S(2)}) copy-start(f32[6,6]{1,0:T(8,128)} %refs_8_.1) | copy-start | bytes 436
  1.3 0.7 %copy-start.3 = (s32[8]{0:T(128)S(1)}, s32[8]{0:T(128)}, u32[]{:S(2)}) copy-start(s32[8]{0:T(128)} %refs_10_.1) | copy-start | bytes 100
  2.0 0.7 %copy-start = (f32[7,6,6]{2,0,1:T(8,128)S(1)}, f32[7,6,6]{2,0,1:T(8,128)}, u32[]{:S(2)}) copy-start(f32[7,6,6]{2,0,1:T(8,128)} %param.17) | copy-start | bytes 3028
  2.7 0.7 %copy-start.1 = (f32[7,6,6]{2,0,1:T(8,128)S(1)}, f32[7,6,6]{2,0,1:T(8,128)}, u32[]{:S(2)}) copy-start(f32[7,6,6]{2,0,1:T(8,128)} %param.18) | copy-start | bytes 3028
  29.5 1.8 %copy-start.4 = (f32[768,128]{1,0:T(8,128)S(1)}, f32[768,128]{1,0:T(8,128)}, u32[]{:S(2)}) copy-start(f32[768,128]{1,0:T(8,128)} %get-tuple-element.5) | copy-start | bytes 1179652
where the time goes:
time: 32.4 us; the launch traced here: 32.1 us
  Pallas kernels  26.1 us (81%)
  local copies, waits for them, and re-layouts  4.72 us (15%)
  between operations  1.32 us (4%)
    pallas_call x1, Pallas kernels, per_device(): pl.pallas_call(functools.partial(kernel, fields, cp, cs, ca, npass, nspan...  26.1 us
    unnamed x12, local copies, waits for them, and re-layouts  4.72 us

commit v1 on v0

v1 whole, which is shorter than its diff:
```python
import functools

import jax
import jax.numpy as jnp
from jax import lax
from jax.experimental import pallas as pl
from jax.experimental.pallas import tpu as pltpu
from jax.sharding import PartitionSpec as P

ITERS = 3
RELAX = 0.8
MESH = pl.DeviceIdType.MESH
F32 = jnp.float32
BF16 = jnp.bfloat16
ROTOR, STATOR = 0, 1
SLOT = 16


def split(x):
    hi = x.astype(BF16)
    lo = (x - hi.astype(F32)).astype(BF16)
    return hi, lo


def kernel(fields, cp, cs, ca, npass, nspan, *refs):
    it = iter(refs)

    def take(n):
        return [next(it) for _ in range(n)]

    psi_in = take(2)
    rhs_in = take(2)
    kap_in = take(2)
    small_in = take(4)
    (counts,) = take(1)
    outs = take(2)
    psi = [take(ITERS) + [outs[r]] for r in range(2)]
    rhs = take(2)
    coef = take(2)
    cen = [take(2) for _ in range(2)]
    ext = [take(2) for _ in range(2)]
    mat = take(2)
    small = take(4)
    blocks, (iface, source) = small[:2], small[2:]
    (precv, ssend, srecv, fsend) = take(4)
    frecv = take(ITERS)
    (in_sem, hs_sem, hr_sem, fs_sem, fr_sem) = take(5)

    nb = fields * cs
    kx = 2 * nb + 16
    plane = cp * cs
    others = npass * nspan - 1

    ip = lax.axis_index("passage")
    js = lax.axis_index("span")
    right = lax.rem(ip + 1, npass)
    left = lax.rem(ip + npass - 1, npass)
    has_next, has_prev = js < nspan - 1, js > 0

    def peer(o):
        return lax.rem(ip + o // nspan, npass), lax.rem(js + o % nspan, nspan)

    def each_peer(body):
        unroll = others if others < 64 else 1
        pl.loop(1, others + 1, unroll=unroll)(body)

    barrier = pltpu.get_barrier_semaphore()
    each_peer(
        lambda o: pl.semaphore_signal(barrier, inc=1, device_id=peer(o), device_id_type=MESH)
    )

    pairs = [
        (psi_in[0], psi[0][0]),
        (psi_in[1], psi[1][0]),
        *zip(small_in, small),
        (kap_in[0], coef[0]),
        (kap_in[1], coef[1]),
        (rhs_in[0], rhs[0]),
        (rhs_in[1], rhs[1]),
    ]
    loads = [pltpu.make_async_copy(a, b, in_sem.at[n]) for n, (a, b) in enumerate(pairs)]
    for c in loads:
        c.start()

    for d, met in ((0, has_prev), (1, has_next)):

        @pl.when(jnp.logical_not(met))
        def _(d=d):
            for r in range(2):
                for k in range(ITERS):
                    srecv[r, k, d] = jnp.zeros((fields, cp, ca), F32)

    def halo_copies(r, k):
        made = []
        for d, p, target in ((0, cp - 1, (right, js)), (1, 0, (left, js))):
            made.append(
                pltpu.make_async_remote_copy(
                    src_ref=psi[r][k].at[:, pl.ds(p * cs, cs), :],
                    dst_ref=precv.at[r, k, d],
                    send_sem=hs_sem.at[r, k, d],
                    recv_sem=hr_sem.at[r, k, d],
                    device_id=target,
                    device_id_type=MESH,
                )
            )
        for d, target in (
            (0, (ip, lax.rem(js + 1, nspan))),
            (1, (ip, lax.rem(js + nspan - 1, nspan))),
        ):
            made.append(
                pltpu.make_async_remote_copy(
                    src_ref=ssend.at[r, k, d],
                    dst_ref=srecv.at[r, k, d],
                    send_sem=hs_sem.at[r, k, 2 + d],
                    recv_sem=hr_sem.at[r, k, 2 + d],
                    device_id=target,
                    device_id_type=MESH,
                )
            )
        return made

    halos = {(r, k): halo_copies(r, k) for r in range(2) for k in range(ITERS)}

    def edge(s):
        return pl.ds(s, cp, stride=cs)

    def pack_span(r, k):
        for d, s in ((0, cs - 1), (1, 0)):
            for f in range(fields):
                ssend[r, k, d, f] = psi[r][k][f, edge(s), :]

    def start_halos(r, k):
        to_right, to_left, to_next, to_prev = halos[r, k]
        to_right.start()
        to_left.start()

        @pl.when(has_next)
        def _():
            to_next.start()

        @pl.when(has_prev)
        def _():
            to_prev.start()

    def finish_sends(r, k):
        to_right, to_left, to_next, to_prev = halos[r, k]
        to_right.wait_send()
        to_left.wait_send()

        @pl.when(has_next)
        def _():
            to_next.wait_send()

        @pl.when(has_prev)
        def _():
            to_prev.wait_send()

    def receive_halos(r, k):
        to_right, to_left, to_next, to_prev = halos[r, k]

        @pl.when(has_prev)
        def _():
            to_next.wait_recv()

        @pl.when(has_next)
        def _():
            to_prev.wait_recv()

        to_right.wait_recv()
        to_left.wait_recv()

    def mix(block, f, parts):
        acc = block(f, 0) * parts[0]
        for g in range(1, fields):
            acc = acc + block(f, g) * parts[g]
        return acc

    def add_halos(r, k):
        new = psi[r][k + 1]
        for d, p in ((0, 0), (1, cp - 1)):
            rows = pl.ds(p * cs, cs)
            c = coef[r][rows, :]
            parts = [precv[r, k, d, g] for g in range(fields)]
            for f in range(fields):
                acc = mix(lambda a, b: blocks[r][a, 1 + d, b], f, parts)
                new[f, rows, :] = new[f, rows, :] + c * acc
        for d, s in ((0, 0), (1, cs - 1)):
            c = coef[r][edge(s), :]
            parts = [srecv[r, k, d, g] for g in range(fields)]
            for f in range(fields):
                acc = mix(lambda a, b: blocks[r][a, 3 + d, b], f, parts)
                new[f, edge(s), :] = new[f, edge(s), :] + c * acc

    lane = lax.broadcasted_iota(jnp.int32, (cs, ca), 1)
    at_slot = lane - SLOT * lax.broadcasted_iota(jnp.int32, (cs, ca), 0)
    wide = lax.broadcasted_iota(jnp.int32, (nb, ca), 1)

    def face_copy(k, o):
        return pltpu.make_async_remote_copy(
            src_ref=fsend.at[k],
            dst_ref=frecv[k].at[o],
            send_sem=fs_sem.at[k],
            recv_sem=fr_sem.at[k],
            device_id=peer(o),
            device_id_type=MESH,
        )

    def pick(x):
        return jnp.sum(x, axis=1, keepdims=True)

    def pack_face(k):
        state = psi[ROTOR][k]
        count = counts[0]
        weights = [jnp.where(p < count, 1.0, 0.0).astype(F32) for p in range(cp)]
        sums = []
        for f in range(fields):
            acc = weights[0] * state[f, pl.ds(0, cs), :]
            for p in range(1, cp):
                acc = acc + weights[p] * state[f, pl.ds(p * cs, cs), :]
            sums.append(jnp.where(lane == ca - 1, acc, 0.0))
        tile = jnp.where(at_slot == fields, jnp.clip(count, 0, cp).astype(F32), 0.0)
        for f in range(fields):
            mixed = mix(lambda a, b: iface[a, b], f, sums)
            tile = jnp.where(at_slot == f, pick(mixed), tile)
        row = jnp.sum(tile, axis=0, keepdims=True)
        fsend[k] = row
        frecv[k][0] = row

    def start_face(k):
        each_peer(lambda o: face_copy(k, o).start())

    def all_faces(k):
        return pltpu.make_async_copy(
            frecv[k].at[pl.ds(1, others)], frecv[k].at[pl.ds(1, others)], fr_sem.at[k]
        )

    def sent_faces(k):
        return pltpu.make_async_copy(
            frecv[k].at[pl.ds(1, others)], frecv[k].at[pl.ds(1, others)], fs_sem.at[k]
        )

    def add_inlet(k):
        all_faces(k).wait()
        away = lax.rem(js - source[js] + nspan, nspan)
        total = frecv[k][away]
        for o in range(1, npass):
            total = total + frecv[k][o * nspan + away]
        total = jnp.broadcast_to(total, (cs, ca))
        count = pick(jnp.where(at_slot == fields, total, 0.0))
        for f in range(fields):
            value = pick(jnp.where(at_slot == f, total, 0.0)) / count
            value = jnp.where(lane == 0, value, 0.0)
            new = psi[STATOR][k + 1]
            for p in range(cp):
                rows = pl.ds(p * cs, cs)
                new[f, rows, :] = new[f, rows, :] + coef[STATOR][rows, :] * value

    def build_matrix(r):
        kk = 5 * nb + 16
        col = lax.broadcasted_iota(jnp.int32, (cs, kk), 1)
        row = lax.broadcasted_iota(jnp.int32, (cs, kk), 0)
        part = col // nb
        g_in = (col - part * nb) // cs
        s_in = col - part * nb - g_in * cs
        which = jnp.full((cs, kk), -1, jnp.int32)
        same = s_in == row
        which = jnp.where((part == 0) & same, 1, which)
        which = jnp.where((part == 2) & same, 2, which)
        which = jnp.where((part == 3) & same, 5, which)
        which = jnp.where((part == 4) & same, 6, which)
        which = jnp.where((part == 1) & (s_in + 1 == row), 3, which)
        which = jnp.where((part == 1) & (s_in == row + 1), 4, which)
        code = jnp.where(which >= 0, which * 8 + g_in, -1)
        middle = jnp.where((part == 1) & same, g_in, -1)
        near, main = [], []
        masks = [[code == (b * 8 + g) for g in range(fields)] for b in range(1, 7)]
        centre = [middle == g for g in range(fields)]
        for f in range(fields):
            acc = jnp.zeros((cs, kk), F32)
            mid = jnp.zeros((cs, kk), F32)
            for g in range(fields):
                mid = jnp.where(centre[g], -RELAX * blocks[r][f, 0, g], mid)
                for b in range(1, 7):
                    acc = jnp.where(masks[b - 1][g], blocks[r][f, b, g], acc)
            near.append(acc)
            main.append(mid)
        hi, lo = split(jnp.concatenate(near + main, axis=0))
        mat[r][pl.ds(0, 2 * nb), :] = hi
        mat[r][pl.ds(2 * nb, 2 * nb), :] = lo

    def clear(r):
        for n in range(2):
            cen[r][n][pl.ds(0, nb), :] = jnp.zeros((nb, ca), BF16)
            cen[r][n][pl.ds((cp + 1) * nb, nb), :] = jnp.zeros((nb, ca), BF16)
            for p in range(cp):
                ext[r][n][pl.ds(p * kx + 2 * nb, 16), :] = jnp.zeros((16, ca), BF16)

    def cell(ref, p):
        return jnp.concatenate([ref[f, pl.ds(p * cs, cs), :] for f in range(fields)], axis=0)

    def store_split(r, k, p):
        new = cell(psi[r][k], p)
        before = jnp.where(wide == 0, 0.0, pltpu.roll(new, 1, 1))
        after = jnp.where(wide == ca - 1, 0.0, pltpu.roll(new, ca - 1, 1))
        for buf, at, value in (
            (cen, (p + 1) * nb, new),
            (ext, p * kx, before),
            (ext, p * kx + nb, after),
        ):
            hi, lo = split(value)
            buf[r][0][pl.ds(at, nb), :] = hi
            buf[r][1][pl.ds(at, nb), :] = lo

    def columns(r, n, p):
        return jnp.concatenate(
            [cen[r][n][pl.ds(p * nb, 3 * nb), :], ext[r][n][pl.ds(p * kx, kx), :]], axis=0
        )

    def interior(r, k):
        for p in range(cp):
            store_split(r, k, p)
        for q in range(cp // 2):
            cells = (2 * q, 2 * q + 1)
            hi = jnp.concatenate([columns(r, 0, p) for p in cells], axis=1)
            lo = jnp.concatenate([columns(r, 1, p) for p in cells], axis=1)
            first = jnp.dot(mat[r][...], hi, preferred_element_type=F32)
            second = jnp.dot(mat[r][pl.ds(0, 2 * nb), :], lo, preferred_element_type=F32)
            both = first[: 2 * nb] + (first[2 * nb :] + second)
            for n, p in enumerate(cells):
                mine = both[:, n * ca : (n + 1) * ca]
                c = coef[r][pl.ds(p * cs, cs), :]
                c = jnp.concatenate([c] * fields, axis=0)
                new = (cell(psi[r][k], p) + mine[nb:]) + c * (cell(rhs[r], p) + mine[:nb])
                for f in range(fields):
                    psi[r][k + 1][f, pl.ds(p * cs, cs), :] = new[f * cs : (f + 1) * cs]

    for c in loads[:2]:
        c.wait()
    for r in range(2):
        pack_span(r, 0)
    for c in loads[2:6]:
        c.wait()
    pack_face(0)
    pl.semaphore_wait(barrier, others)
    start_halos(ROTOR, 0)
    start_face(0)
    start_halos(STATOR, 0)

    for r in range(2):
        clear(r)
        build_matrix(r)
    for c in loads[6:]:
        c.wait()
    for r in range(2):
        coef[r][...] = RELAX / coef[r][...]
    interior(ROTOR, 0)
    interior(STATOR, 0)

    for k in range(ITERS):
        more = k + 1 < ITERS
        receive_halos(ROTOR, k)
        add_halos(ROTOR, k)
        if more:
            pack_span(ROTOR, k + 1)
            start_halos(ROTOR, k + 1)
            pack_face(k + 1)
            start_face(k + 1)
            interior(ROTOR, k + 1)
        receive_halos(STATOR, k)
        add_halos(STATOR, k)
        add_inlet(k)
        if more:
            pack_span(STATOR, k + 1)
            start_halos(STATOR, k + 1)
            interior(STATOR, k + 1)

    for k in range(ITERS):
        for r in range(2):
            finish_sends(r, k)
        sent_faces(k).wait()


def write_out(*refs):
    srcs, dsts, sem = refs[:2], refs[2:4], refs[4]
    copies = [pltpu.make_async_copy(srcs[n], dsts[n], sem.at[n]) for n in range(2)]
    for c in copies:
        c.start()
    for c in copies:
        c.wait()


def per_device(
    npass,
    nspan,
    psi_rotor,
    psi_stator,
    rhs_rotor,
    rhs_stator,
    kappa_rotor,
    kappa_stator,
    rotor_blocks,
    stator_blocks,
    interface_block,
    pass_counts,
    tile_source,
):
    fields, cp, cs, ca = psi_rotor.shape
    shape = (fields, cp * cs, ca)
    flat = [x.reshape(shape) for x in (psi_rotor, psi_stator, rhs_rotor, rhs_stator)]
    kaps = [x.reshape(cp * cs, ca) for x in (kappa_rotor, kappa_stator)]
    small = [x.transpose(1, 0, 2) for x in (rotor_blocks, stator_blocks)]
    small += [interface_block, tile_source]
    nb = fields * cs
    kx = 2 * nb + 16
    state = pltpu.VMEM(shape, F32)
    scratch = [state] * (2 * ITERS)
    scratch += [state] * 2
    scratch += [pltpu.VMEM((cp * cs, ca), F32)] * 2
    scratch += [pltpu.VMEM(((cp + 2) * nb, ca), BF16)] * 4
    scratch += [pltpu.VMEM((cp * kx, ca), BF16)] * 4
    scratch += [pltpu.VMEM((4 * nb, 5 * nb + 16), BF16)] * 2
    scratch += [pltpu.SMEM(x.shape, x.dtype) for x in small]
    scratch += [
        pltpu.VMEM((2, ITERS, 2, fields, cs, ca), F32),
        pltpu.VMEM((2, ITERS, 2, fields, cp, ca), F32),
        pltpu.VMEM((2, ITERS, 2, fields, cp, ca), F32),
        pltpu.VMEM((ITERS, 1, ca), F32),
    ]
    scratch += [pltpu.VMEM((npass * nspan, 1, ca), F32)] * ITERS
    dma = pltpu.SemaphoreType.DMA
    scratch += [
        dma((10,)),
        dma((2, ITERS, 4)),
        dma((2, ITERS, 4)),
        dma((ITERS,)),
        dma((ITERS,)),
    ]
    hbm = pl.BlockSpec(memory_space=pltpu.HBM)
    vmem = pl.BlockSpec(memory_space=pltpu.VMEM)
    done = pl.pallas_call(
        functools.partial(kernel, fields, cp, cs, ca, npass, nspan),
        out_shape=[pltpu.VMEM(shape, F32)] * 2,
        in_specs=[hbm] * 10 + [pl.BlockSpec(memory_space=pltpu.SMEM)],
        out_specs=[vmem] * 2,
        scratch_shapes=scratch,
        compiler_params=pltpu.CompilerParams(
            collective_id=0, has_side_effects=True, vmem_limit_bytes=32 * 1024 * 1024
        ),
    )(*[pltpu.with_memory_space_constraint(x, pltpu.HBM) for x in flat + kaps + small], pass_counts)
    out = pl.pallas_call(
        write_out,
        out_shape=[pltpu.HBM(shape, F32)] * 2,
        in_specs=[vmem] * 2,
        out_specs=[hbm] * 2,
        scratch_shapes=[dma((2,))],
    )(*[pltpu.with_memory_space_constraint(x, pltpu.VMEM) for x in done])
    return tuple(x.reshape(psi_rotor.shape) for x in out)


def solution(mesh):
    return jax.shard_map(
        functools.partial(per_device, mesh.shape["passage"], mesh.shape["span"]),
        mesh=mesh,
        in_specs=(
            P(None, "passage", "span", None),
            P(None, "passage", "span", None),
            P(None, "passage", "span", None),
            P(None, "passage", "span", None),
            P("passage", "span", None),
            P("passage", "span", None),
            P(),
            P(),
            P(),
            P("passage"),
            P(),
        ),
        out_specs=(P(None, "passage", "span", None), P(None, "passage", "span", None)),
        check_vma=False,
    )
```

time: 32.4 us -> 22.7 us (0.70)
  Pallas kernels: 26.1 us -> 21.3 us
  local copies, waits for them, and re-layouts: 4.72 us -> 0 us
    pallas_call x1, Pallas kernels: 26.1 us -> 20.4 us  [per_device(): pl.pallas_call(functools.partial(kernel, fields, cp, cs, ca, npass, nspan...]
    unnamed x12 -> x0, local copies, waits for them, and re-layouts: 4.72 us -> none
    pallas_call x0 -> x1, Pallas kernels: none -> 0.89 us  [per_device(): pl.pallas_call(write_out, out_shape=[pltpu.HBM(shape, F32)] * 2, in_specs...]
where the time goes in v1:
time: 22.7 us; the launch traced here: 22.6 us
  Pallas kernels  21.3 us (94%)
  between operations  1.29 us (6%)
    pallas_call x1, Pallas kernels, per_device(): pl.pallas_call(functools.partial(kernel, fields, cp, cs, ca, npass, nspan...  20.4 us
    pallas_call x1, Pallas kernels, per_device(): pl.pallas_call(write_out, out_shape=[pltpu.HBM(shape, F32)] * 2, in_specs...  0.89 us

profile of v1, /device:TPU:0, one launch (start us, length us, event | category | flops | bytes accessed | tf_op | source)
XLA Modules:
  0.0 22.6 jit_solution(17692009525173218926)
XLA Ops:
  1.3 20.4 %shard_map.122 = (f32[6,128,128]{2,1,0:T(8,128)S(1)}, f32[6,128,128]{2,1,0:T(8,128)S(1)}) custom-call(f32[6,128,128]{2,1,0:T(8,128)} %bitcast.10, f32[6,128,128]{2,1,0:T(8,128)} %bitcast.11, f32[6,128,128]{2,1,0:T(8,128)} %bitcast.12, f32[6,128,128]{2,1,0:T(8,128)} %bitcast.13, f32[128,128]{1,0:T(8,128)} %bitcast.14, f32[128,128]{1,0:T(8,128)} %bitcast.15, ...), custom_call_target="tpu_custom_call" | custom-call | tf_op jit(solution)/shard_map/pallas_call | solution.py:440
  21.7 0.9 %shard_map.123 = (f32[6,128,128]{2,1,0:T(8,128)}, f32[6,128,128]{2,1,0:T(8,128)}) custom-call(f32[6,128,128]{2,1,0:T(8,128)S(1)} %get-tuple-element.6.refs_0_, f32[6,128,128]{2,1,0:T(8,128)S(1)} %get-tuple-element.7.refs_1_), custom_call_target="tpu_custom_call" | custom-call | tf_op jit(solution)/shard_map/pallas_call | solution.py:450

commit v2 on v1

--- a/solution.py
+++ b/solution.py
@@ -42,9 +42,9 @@
     mat = take(2)
     small = take(4)
     blocks, (iface, source) = small[:2], small[2:]
-    (precv, ssend, srecv, fsend) = take(4)
+    (precv, psend, ssend, srecv, fsend, pcor, scor) = take(7)
     frecv = take(ITERS)
-    (in_sem, hs_sem, hr_sem, fs_sem, fr_sem) = take(5)
+    (in_sem, hs_sem, hr_sem, fs_sem, fr_sem, gate) = take(6)
 
     nb = fields * cs
     kx = 2 * nb + 16
@@ -64,17 +64,12 @@
         unroll = others if others < 64 else 1
         pl.loop(1, others + 1, unroll=unroll)(body)
 
-    barrier = pltpu.get_barrier_semaphore()
-    each_peer(
-        lambda o: pl.semaphore_signal(barrier, inc=1, device_id=peer(o), device_id_type=MESH)
-    )
-
     pairs = [
         (psi_in[0], psi[0][0]),
-        (psi_in[1], psi[1][0]),
+        (psi_in[1], psi[1][0].at[pl.ds(0, fields)]),
+        (kap_in[1], psi[STATOR][0].at[fields]),
         *zip(small_in, small),
         (kap_in[0], coef[0]),
-        (kap_in[1], coef[1]),
         (rhs_in[0], rhs[0]),
         (rhs_in[1], rhs[1]),
     ]
@@ -82,21 +77,35 @@
     for c in loads:
         c.start()
 
+    barrier = pltpu.get_barrier_semaphore()
+    for o in range(1, npass):
+        pl.semaphore_signal(
+            barrier, inc=1, device_id=(lax.rem(ip + o, npass), js), device_id_type=MESH
+        )
+    for o in range(1, nspan):
+        pl.semaphore_signal(
+            barrier, inc=1, device_id=(ip, lax.rem(js + o, nspan)), device_id_type=MESH
+        )
+
     for d, met in ((0, has_prev), (1, has_next)):
 
         @pl.when(jnp.logical_not(met))
         def _(d=d):
             for r in range(2):
                 for k in range(ITERS):
-                    srecv[r, k, d] = jnp.zeros((fields, cp, ca), F32)
+                    srecv[r, k, d, pl.ds(0, fields)] = jnp.zeros((fields, cp, ca), F32)
+                    srecv[r, k, d, fields] = jnp.ones((cp, ca), F32)
 
     def halo_copies(r, k):
         made = []
+        n = fields + 1 if (r, k) == (STATOR, 0) else fields
         for d, p, target in ((0, cp - 1, (right, js)), (1, 0, (left, js))):
             made.append(
                 pltpu.make_async_remote_copy(
-                    src_ref=psi[r][k].at[:, pl.ds(p * cs, cs), :],
-                    dst_ref=precv.at[r, k, d],
+                    src_ref=psend.at[d]
+                    if (r, k) == (STATOR, 1)
+                    else psi[r][k].at[:, pl.ds(p * cs, cs), :],
+                    dst_ref=precv.at[r, k, d, pl.ds(0, n)],
                     send_sem=hs_sem.at[r, k, d],
                     recv_sem=hr_sem.at[r, k, d],
                     device_id=target,
@@ -109,8 +118,8 @@
         ):
             made.append(
                 pltpu.make_async_remote_copy(
-                    src_ref=ssend.at[r, k, d],
-                    dst_ref=srecv.at[r, k, d],
+                    src_ref=ssend.at[r, k, d, pl.ds(0, n)],
+                    dst_ref=srecv.at[r, k, d, pl.ds(0, n)],
                     send_sem=hs_sem.at[r, k, 2 + d],
                     recv_sem=hr_sem.at[r, k, 2 + d],
                     device_id=target,
@@ -126,8 +135,13 @@
 
     def pack_span(r, k):
         for d, s in ((0, cs - 1), (1, 0)):
+            for f in range(psi[r][k].shape[0]):
+                ssend[r, k, d, f] = psi[r][k][f, edge(s), :]
+
+    def pack_pitch(r, k):
+        for d, p in ((0, cp - 1), (1, 0)):
             for f in range(fields):
-                ssend[r, k, d, f] = psi[r][k][f, edge(s), :]
+                psend[d, f] = psi[r][k][f, pl.ds(p * cs, cs), :]
 
     def start_halos(r, k):
         to_right, to_left, to_next, to_prev = halos[r, k]
@@ -181,12 +195,16 @@
             rows = pl.ds(p * cs, cs)
             c = coef[r][rows, :]
             parts = [precv[r, k, d, g] for g in range(fields)]
+            if (r, k) == (STATOR, 1):
+                parts = [x + pcor[d, g] for g, x in enumerate(parts)]
             for f in range(fields):
                 acc = mix(lambda a, b: blocks[r][a, 1 + d, b], f, parts)
                 new[f, rows, :] = new[f, rows, :] + c * acc
         for d, s in ((0, 0), (1, cs - 1)):
             c = coef[r][edge(s), :]
             parts = [srecv[r, k, d, g] for g in range(fields)]
+            if (r, k) == (STATOR, 1):
+                parts = [x + scor[d, g] for g, x in enumerate(parts)]
             for f in range(fields):
                 acc = mix(lambda a, b: blocks[r][a, 3 + d, b], f, parts)
                 new[f, edge(s), :] = new[f, edge(s), :] + c * acc
@@ -239,21 +257,42 @@
             frecv[k].at[pl.ds(1, others)], frecv[k].at[pl.ds(1, others)], fs_sem.at[k]
         )
 
-    def add_inlet(k):
-        all_faces(k).wait()
-        away = lax.rem(js - source[js] + nspan, nspan)
+    def inlets(k, at):
+        away = lax.rem(js - source[at] + nspan, nspan)
         total = frecv[k][away]
         for o in range(1, npass):
             total = total + frecv[k][o * nspan + away]
         total = jnp.broadcast_to(total, (cs, ca))
         count = pick(jnp.where(at_slot == fields, total, 0.0))
+        made = []
         for f in range(fields):
             value = pick(jnp.where(at_slot == f, total, 0.0)) / count
-            value = jnp.where(lane == 0, value, 0.0)
-            new = psi[STATOR][k + 1]
+            made.append(jnp.where(lane == 0, value, 0.0))
+        return made
+
+    def add_inlet(k):
+        all_faces(k).wait()
+        new = psi[STATOR][k + 1]
+        values = inlets(k, js)
+        for f in range(fields):
             for p in range(cp):
                 rows = pl.ds(p * cs, cs)
-                new[f, rows, :] = new[f, rows, :] + coef[STATOR][rows, :] * value
+                new[f, rows, :] = new[f, rows, :] + coef[STATOR][rows, :] * values[f]
+        return values
+
+    def neighbour_inlets(own):
+        for d in range(2):
+            c = RELAX / precv[STATOR, 0, d, fields]
+            for f in range(fields):
+                pcor[d, f] = c * own[f]
+        for d, s, at, met in (
+            (0, cs - 1, jnp.maximum(js - 1, 0), has_prev),
+            (1, 0, jnp.minimum(js + 1, nspan - 1), has_next),
+        ):
+            c = jnp.where(met, 1.0, 0.0) * (RELAX / srecv[STATOR, 0, d, fields])
+            values = inlets(0, at)
+            for f in range(fields):
+                scor[d, f] = c * jnp.broadcast_to(values[f][s : s + 1], (cp, ca))
 
     def build_matrix(r):
         kk = 5 * nb + 16
@@ -334,45 +373,69 @@
                 for f in range(fields):
                     psi[r][k + 1][f, pl.ds(p * cs, cs), :] = new[f * cs : (f + 1) * cs]
 
-    for c in loads[:2]:
+    loads[0].wait()
+    pack_span(ROTOR, 0)
+    pl.semaphore_wait(barrier, npass + nspan - 2)
+    start_halos(ROTOR, 0)
+    for o in range(1, npass):
+        pl.semaphore_signal(
+            gate, inc=1, device_id=(lax.rem(ip + o, npass), js), device_id_type=MESH
+        )
+    for c in loads[1:3]:
         c.wait()
-    for r in range(2):
-        pack_span(r, 0)
-    for c in loads[2:6]:
+    pack_span(STATOR, 0)
+    start_halos(STATOR, 0)
+    for c in loads[3:7]:
         c.wait()
     pack_face(0)
-    pl.semaphore_wait(barrier, others)
-    start_halos(ROTOR, 0)
+    pl.semaphore_wait(gate, npass - 1)
     start_face(0)
-    start_halos(STATOR, 0)
 
     for r in range(2):
         clear(r)
         build_matrix(r)
-    for c in loads[6:]:
+    for c in loads[7:]:
         c.wait()
-    for r in range(2):
-        coef[r][...] = RELAX / coef[r][...]
+    coef[ROTOR][...] = RELAX / coef[ROTOR][...]
+    coef[STATOR][...] = RELAX / psi[STATOR][0][fields]
     interior(ROTOR, 0)
     interior(STATOR, 0)
 
-    for k in range(ITERS):
-        more = k + 1 < ITERS
-        receive_halos(ROTOR, k)
-        add_halos(ROTOR, k)
-        if more:
-            pack_span(ROTOR, k + 1)
-            start_halos(ROTOR, k + 1)
-            pack_face(k + 1)
-            start_face(k + 1)
-            interior(ROTOR, k + 1)
-        receive_halos(STATOR, k)
-        add_halos(STATOR, k)
-        add_inlet(k)
-        if more:
-            pack_span(STATOR, k + 1)
-            start_halos(STATOR, k + 1)
-            interior(STATOR, k + 1)
+    receive_halos(ROTOR, 0)
+    add_halos(ROTOR, 0)
+    pack_span(ROTOR, 1)
+    start_halos(ROTOR, 1)
+    pack_face(1)
+    start_face(1)
+    receive_halos(STATOR, 0)
+    add_halos(STATOR, 0)
+    pack_span(STATOR, 1)
+    pack_pitch(STATOR, 1)
+    start_halos(STATOR, 1)
+    interior(ROTOR, 1)
+
+    receive_halos(ROTOR, 1)
+    add_halos(ROTOR, 1)
+    pack_face(2)
+    start_face(2)
+    pack_span(ROTOR, 2)
+    start_halos(ROTOR, 2)
+    own = add_inlet(0)
+    neighbour_inlets(own)
+    interior(STATOR, 1)
+    receive_halos(STATOR, 1)
+    add_halos(STATOR, 1)
+    add_inlet(1)
+    pack_span(STATOR, 2)
+    start_halos(STATOR, 2)
+    interior(ROTOR, 2)
+    interior(STATOR, 2)
+
+    receive_halos(ROTOR, 2)
+    add_halos(ROTOR, 2)
+    receive_halos(STATOR, 2)
+    add_halos(STATOR, 2)
+    add_inlet(2)
 
     for k in range(ITERS):
         for r in range(2):
@@ -413,7 +476,9 @@
     nb = fields * cs
     kx = 2 * nb + 16
     state = pltpu.VMEM(shape, F32)
-    scratch = [state] * (2 * ITERS)
+    scratch = [state] * ITERS
+    scratch += [pltpu.VMEM((fields + 1, cp * cs, ca), F32)]
+    scratch += [state] * (ITERS - 1)
     scratch += [state] * 2
     scratch += [pltpu.VMEM((cp * cs, ca), F32)] * 2
     scratch += [pltpu.VMEM(((cp + 2) * nb, ca), BF16)] * 4
@@ -421,10 +486,13 @@
     scratch += [pltpu.VMEM((4 * nb, 5 * nb + 16), BF16)] * 2
     scratch += [pltpu.SMEM(x.shape, x.dtype) for x in small]
     scratch += [
-        pltpu.VMEM((2, ITERS, 2, fields, cs, ca), F32),
-        pltpu.VMEM((2, ITERS, 2, fields, cp, ca), F32),
-        pltpu.VMEM((2, ITERS, 2, fields, cp, ca), F32),
+        pltpu.VMEM((2, ITERS, 2, fields + 1, cs, ca), F32),
+        pltpu.VMEM((2, fields, cs, ca), F32),
+        pltpu.VMEM((2, ITERS, 2, fields + 1, cp, ca), F32),
+        pltpu.VMEM((2, ITERS, 2, fields + 1, cp, ca), F32),
         pltpu.VMEM((ITERS, 1, ca), F32),
+        pltpu.VMEM((2, fields, cs, ca), F32),
+        pltpu.VMEM((2, fields, cp, ca), F32),
     ]
     scratch += [pltpu.VMEM((npass * nspan, 1, ca), F32)] * ITERS
     dma = pltpu.SemaphoreType.DMA
@@ -434,6 +502,7 @@
         dma((2, ITERS, 4)),
         dma((ITERS,)),
         dma((ITERS,)),
+        pltpu.SemaphoreType.REGULAR,
     ]
     hbm = pl.BlockSpec(memory_space=pltpu.HBM)
     vmem = pl.BlockSpec(memory_space=pltpu.VMEM)

time: 22.7 us -> 22 us (0.969)
  Pallas kernels: 21.3 us -> 20.6 us
    pallas_call x1, Pallas kernels: 20.4 us -> 19.7 us  [per_device(): pl.pallas_call(functools.partial(kernel, fields, cp, cs, ca, npass, nspan...]
where the time goes in v2:
time: 22 us; the launch traced here: 21.8 us
  Pallas kernels  20.6 us (94%)
  between operations  1.29 us (6%)
    pallas_call x1, Pallas kernels, per_device(): pl.pallas_call(functools.partial(kernel, fields, cp, cs, ca, npass, nspan...  19.7 us
    pallas_call x1, Pallas kernels, per_device(): pl.pallas_call(write_out, out_shape=[pltpu.HBM(shape, F32)] * 2, in_specs...  0.89 us

profile of v2, /device:TPU:0, one launch (start us, length us, event | category | flops | bytes accessed | tf_op | source)
XLA Modules:
  0.0 21.8 jit_solution(14692878392083007136)
XLA Ops:
  1.3 19.7 %shard_map.122 = (f32[6,128,128]{2,1,0:T(8,128)S(1)}, f32[6,128,128]{2,1,0:T(8,128)S(1)}) custom-call(f32[6,128,128]{2,1,0:T(8,128)} %bitcast.10, f32[6,128,128]{2,1,0:T(8,128)} %bitcast.11, f32[6,128,128]{2,1,0:T(8,128)} %bitcast.12, f32[6,128,128]{2,1,0:T(8,128)} %bitcast.13, f32[128,128]{1,0:T(8,128)} %bitcast.14, f32[128,128]{1,0:T(8,128)} %bitcast.15, ...), custom_call_target="tpu_custom_call" | custom-call | tf_op jit(solution)/shard_map/pallas_call | solution.py:509
  20.9 0.9 %shard_map.123 = (f32[6,128,128]{2,1,0:T(8,128)}, f32[6,128,128]{2,1,0:T(8,128)}) custom-call(f32[6,128,128]{2,1,0:T(8,128)S(1)} %get-tuple-element.6.refs_0_, f32[6,128,128]{2,1,0:T(8,128)S(1)} %get-tuple-element.7.refs_1_), custom_call_target="tpu_custom_call" | custom-call | tf_op jit(solution)/shard_map/pallas_call | solution.py:519

commit v3 on v2

--- a/solution.py
+++ b/solution.py
@@ -138,15 +138,43 @@
             for f in range(psi[r][k].shape[0]):
                 ssend[r, k, d, f] = psi[r][k][f, edge(s), :]
 
-    def pack_pitch(r, k):
-        for d, p in ((0, cp - 1), (1, 0)):
-            for f in range(fields):
-                psend[d, f] = psi[r][k][f, pl.ds(p * cs, cs), :]
-
-    def start_halos(r, k):
-        to_right, to_left, to_next, to_prev = halos[r, k]
-        to_right.start()
-        to_left.start()
+    def start_pitch(r, k):
+        to_right, to_left = halos[r, k][:2]
+
+        @pl.when(ip == 0)
+        def _():
+            to_left.start()
+            to_right.start()
+
+        @pl.when(ip > 0)
+        def _():
+            to_right.start()
+            to_left.start()
+
+    def start_far(r, k):
+        to_right, to_left = halos[r, k][:2]
+
+        @pl.when(ip == 0)
+        def _():
+            to_left.start()
+
+        @pl.when(ip > 0)
+        def _():
+            to_right.start()
+
+    def start_near(r, k):
+        to_right, to_left = halos[r, k][:2]
+
+        @pl.when(ip == 0)
+        def _():
+            to_right.start()
+
+        @pl.when(ip > 0)
+        def _():
+            to_left.start()
+
+    def start_span(r, k):
+        to_next, to_prev = halos[r, k][2:]
 
         @pl.when(has_next)
         def _():
@@ -168,20 +196,6 @@
         @pl.when(has_prev)
         def _():
             to_prev.wait_send()
-
-    def receive_halos(r, k):
-        to_right, to_left, to_next, to_prev = halos[r, k]
-
-        @pl.when(has_prev)
-        def _():
-            to_next.wait_recv()
-
-        @pl.when(has_next)
-        def _():
-            to_prev.wait_recv()
-
-        to_right.wait_recv()
-        to_left.wait_recv()
 
     def mix(block, f, parts):
         acc = block(f, 0) * parts[0]
@@ -189,17 +203,18 @@
             acc = acc + block(f, g) * parts[g]
         return acc
 
-    def add_halos(r, k):
+    def span_terms(r, k):
         new = psi[r][k + 1]
-        for d, p in ((0, 0), (1, cp - 1)):
-            rows = pl.ds(p * cs, cs)
-            c = coef[r][rows, :]
-            parts = [precv[r, k, d, g] for g in range(fields)]
-            if (r, k) == (STATOR, 1):
-                parts = [x + pcor[d, g] for g, x in enumerate(parts)]
-            for f in range(fields):
-                acc = mix(lambda a, b: blocks[r][a, 1 + d, b], f, parts)
-                new[f, rows, :] = new[f, rows, :] + c * acc
+        to_next, to_prev = halos[r, k][2:]
+
+        @pl.when(has_prev)
+        def _():
+            to_next.wait_recv()
+
+        @pl.when(has_next)
+        def _():
+            to_prev.wait_recv()
+
         for d, s in ((0, 0), (1, cs - 1)):
             c = coef[r][edge(s), :]
             parts = [srecv[r, k, d, g] for g in range(fields)]
@@ -208,6 +223,28 @@
             for f in range(fields):
                 acc = mix(lambda a, b: blocks[r][a, 3 + d, b], f, parts)
                 new[f, edge(s), :] = new[f, edge(s), :] + c * acc
+
+    def add_halos(r, k, send):
+        span_terms(r, k)
+        new = psi[r][k + 1]
+        for d, p in ((0, 0), (1, cp - 1)):
+            rows = pl.ds(p * cs, cs)
+            c = coef[r][rows, :]
+            halos[r, k][d].wait_recv()
+            parts = [precv[r, k, d, g] for g in range(fields)]
+            if (r, k) == (STATOR, 1):
+                parts = [x + pcor[d, g] for g, x in enumerate(parts)]
+            for f in range(fields):
+                acc = mix(lambda a, b: blocks[r][a, 1 + d, b], f, parts)
+                value = new[f, rows, :] + c * acc
+                new[f, rows, :] = value
+                if send and (r, k) == (STATOR, 0):
+                    psend[1 - d, f] = value
+            if send:
+                halos[r, k + 1][1 - d].start()
+        if send:
+            pack_span(r, k + 1)
+            start_span(r, k + 1)
 
     lane = lax.broadcasted_iota(jnp.int32, (cs, ca), 1)
     at_slot = lane - SLOT * lax.broadcasted_iota(jnp.int32, (cs, ca), 0)
@@ -270,14 +307,25 @@
             made.append(jnp.where(lane == 0, value, 0.0))
         return made
 
-    def add_inlet(k):
+    def add_inlet(k, send):
         all_faces(k).wait()
         new = psi[STATOR][k + 1]
         values = inlets(k, js)
-        for f in range(fields):
-            for p in range(cp):
-                rows = pl.ds(p * cs, cs)
+
+        def add(p):
+            rows = pl.ds(p * cs, cs)
+            for f in range(fields):
                 new[f, rows, :] = new[f, rows, :] + coef[STATOR][rows, :] * values[f]
+
+        add(0)
+        add(cp - 1)
+        if send:
+            start_pitch(STATOR, k + 1)
+        for p in range(1, cp - 1):
+            add(p)
+        if send:
+            pack_span(STATOR, k + 1)
+            start_span(STATOR, k + 1)
         return values
 
     def neighbour_inlets(own):
@@ -376,15 +424,19 @@
     loads[0].wait()
     pack_span(ROTOR, 0)
     pl.semaphore_wait(barrier, npass + nspan - 2)
-    start_halos(ROTOR, 0)
+    start_far(ROTOR, 0)
+    for c in loads[1:3]:
+        c.wait()
+    start_far(STATOR, 0)
+    start_near(ROTOR, 0)
+    start_span(ROTOR, 0)
+    start_near(STATOR, 0)
+    pack_span(STATOR, 0)
+    start_span(STATOR, 0)
     for o in range(1, npass):
         pl.semaphore_signal(
             gate, inc=1, device_id=(lax.rem(ip + o, npass), js), device_id_type=MESH
         )
-    for c in loads[1:3]:
-        c.wait()
-    pack_span(STATOR, 0)
-    start_halos(STATOR, 0)
     for c in loads[3:7]:
         c.wait()
     pack_face(0)
@@ -401,46 +453,29 @@
     interior(ROTOR, 0)
     interior(STATOR, 0)
 
-    receive_halos(ROTOR, 0)
-    add_halos(ROTOR, 0)
-    pack_span(ROTOR, 1)
-    start_halos(ROTOR, 1)
+    add_halos(ROTOR, 0, True)
     pack_face(1)
     start_face(1)
-    receive_halos(STATOR, 0)
-    add_halos(STATOR, 0)
-    pack_span(STATOR, 1)
-    pack_pitch(STATOR, 1)
-    start_halos(STATOR, 1)
+    add_halos(STATOR, 0, True)
     interior(ROTOR, 1)
-
-    receive_halos(ROTOR, 1)
-    add_halos(ROTOR, 1)
+    neighbour_inlets(add_inlet(0, False))
+    interior(STATOR, 1)
+
+    add_halos(ROTOR, 1, True)
     pack_face(2)
     start_face(2)
-    pack_span(ROTOR, 2)
-    start_halos(ROTOR, 2)
-    own = add_inlet(0)
-    neighbour_inlets(own)
-    interior(STATOR, 1)
-    receive_halos(STATOR, 1)
-    add_halos(STATOR, 1)
-    add_inlet(1)
-    pack_span(STATOR, 2)
-    start_halos(STATOR, 2)
+    add_halos(STATOR, 1, False)
+    add_inlet(1, True)
     interior(ROTOR, 2)
     interior(STATOR, 2)
-
-    receive_halos(ROTOR, 2)
-    add_halos(ROTOR, 2)
-    receive_halos(STATOR, 2)
-    add_halos(STATOR, 2)
-    add_inlet(2)
 
     for k in range(ITERS):
         for r in range(2):
             finish_sends(r, k)
         sent_faces(k).wait()
+    add_halos(ROTOR, 2, False)
+    add_inlet(2, False)
+    add_halos(STATOR, 2, False)
 
 
 def write_out(*refs):

time: 22 us -> 21.2 us (0.964)
  Pallas kernels: 20.6 us -> 19.7 us
    pallas_call x1, Pallas kernels: 19.7 us -> 18.8 us  [per_device(): pl.pallas_call(functools.partial(kernel, fields, cp, cs, ca, npass, nspan...]
where the time goes in v3:
time: 21.2 us; the launch traced here: 21 us
  Pallas kernels  19.7 us (93%)
  between operations  1.29 us (6%)
    pallas_call x1, Pallas kernels, per_device(): pl.pallas_call(functools.partial(kernel, fields, cp, cs, ca, npass, nspan...  18.8 us
    pallas_call x1, Pallas kernels, per_device(): pl.pallas_call(write_out, out_shape=[pltpu.HBM(shape, F32)] * 2, in_specs...  0.89 us

profile of v3, /device:TPU:0, one launch (start us, length us, event | category | flops | bytes accessed | tf_op | source)
XLA Modules:
  0.0 21.0 jit_solution(16785350493202594279)
XLA Ops:
  1.3 18.8 %shard_map.122 = (f32[6,128,128]{2,1,0:T(8,128)S(1)}, f32[6,128,128]{2,1,0:T(8,128)S(1)}) custom-call(f32[6,128,128]{2,1,0:T(8,128)} %bitcast.10, f32[6,128,128]{2,1,0:T(8,128)} %bitcast.11, f32[6,128,128]{2,1,0:T(8,128)} %bitcast.12, f32[6,128,128]{2,1,0:T(8,128)} %bitcast.13, f32[128,128]{1,0:T(8,128)} %bitcast.14, f32[128,128]{1,0:T(8,128)} %bitcast.15, ...), custom_call_target="tpu_custom_call" | custom-call | tf_op jit(solution)/shard_map/pallas_call | solution.py:544
  20.1 0.9 %shard_map.123 = (f32[6,128,128]{2,1,0:T(8,128)}, f32[6,128,128]{2,1,0:T(8,128)}) custom-call(f32[6,128,128]{2,1,0:T(8,128)S(1)} %get-tuple-element.6.refs_0_, f32[6,128,128]{2,1,0:T(8,128)S(1)} %get-tuple-element.7.refs_1_), custom_call_target="tpu_custom_call" | custom-call | tf_op jit(solution)/shard_map/pallas_call | solution.py:554

commit v4 on v3

--- a/solution.py
+++ b/solution.py
@@ -226,6 +226,7 @@
 
     def add_halos(r, k, send):
         span_terms(r, k)
+        inner = face_sums(k + 1, range(1, cp - 1)) if send and r == ROTOR else None
         new = psi[r][k + 1]
         for d, p in ((0, 0), (1, cp - 1)):
             rows = pl.ds(p * cs, cs)
@@ -245,6 +246,9 @@
         if send:
             pack_span(r, k + 1)
             start_span(r, k + 1)
+        if inner is not None:
+            pack_face(k + 1, inner)
+            start_face(k + 1)
 
     lane = lax.broadcasted_iota(jnp.int32, (cs, ca), 1)
     at_slot = lane - SLOT * lax.broadcasted_iota(jnp.int32, (cs, ca), 0)
@@ -263,16 +267,22 @@
     def pick(x):
         return jnp.sum(x, axis=1, keepdims=True)
 
-    def pack_face(k):
-        state = psi[ROTOR][k]
-        count = counts[0]
-        weights = [jnp.where(p < count, 1.0, 0.0).astype(F32) for p in range(cp)]
+    def face_sums(k, where):
+        weights = [jnp.where(p < counts[0], 1.0, 0.0).astype(F32) for p in where]
         sums = []
         for f in range(fields):
-            acc = weights[0] * state[f, pl.ds(0, cs), :]
-            for p in range(1, cp):
-                acc = acc + weights[p] * state[f, pl.ds(p * cs, cs), :]
-            sums.append(jnp.where(lane == ca - 1, acc, 0.0))
+            parts = [
+                w * psi[ROTOR][k][f, pl.ds(p * cs, cs), :] for w, p in zip(weights, where)
+            ]
+            while len(parts) > 1:
+                parts = [sum(parts[n + 1 : n + 2], parts[n]) for n in range(0, len(parts), 2)]
+            sums.append(parts[0])
+        return sums
+
+    def pack_face(k, inner):
+        count = counts[0]
+        ends = face_sums(k, (0, cp - 1))
+        sums = [jnp.where(lane == ca - 1, a + b, 0.0) for a, b in zip(inner, ends)]
         tile = jnp.where(at_slot == fields, jnp.clip(count, 0, cp).astype(F32), 0.0)
         for f in range(fields):
             mixed = mix(lambda a, b: iface[a, b], f, sums)
@@ -439,7 +449,7 @@
         )
     for c in loads[3:7]:
         c.wait()
-    pack_face(0)
+    pack_face(0, face_sums(0, range(1, cp - 1)))
     pl.semaphore_wait(gate, npass - 1)
     start_face(0)
 
@@ -454,16 +464,12 @@
     interior(STATOR, 0)
 
     add_halos(ROTOR, 0, True)
-    pack_face(1)
-    start_face(1)
     add_halos(STATOR, 0, True)
     interior(ROTOR, 1)
     neighbour_inlets(add_inlet(0, False))
     interior(STATOR, 1)
 
     add_halos(ROTOR, 1, True)
-    pack_face(2)
-    start_face(2)
     add_halos(STATOR, 1, False)
     add_inlet(1, True)
     interior(ROTOR, 2)

time: 21.2 us -> 21.2 us (level)
  no operation moved by 1% of the time
where the time goes in v4:
time: 21.2 us; the launch traced here: 21 us
  Pallas kernels  19.7 us (93%)
  between operations  1.29 us (6%)
    pallas_call x1, Pallas kernels, per_device(): pl.pallas_call(functools.partial(kernel, fields, cp, cs, ca, npass, nspan...  18.8 us
    pallas_call x1, Pallas kernels, per_device(): pl.pallas_call(write_out, out_shape=[pltpu.HBM(shape, F32)] * 2, in_specs...  0.89 us

profile of v4, /device:TPU:0, one launch (start us, length us, event | category | flops | bytes accessed | tf_op | source)
XLA Modules:
  0.0 21.0 jit_solution(210594541212676757)
XLA Ops:
  1.3 18.8 %shard_map.122 = (f32[6,128,128]{2,1,0:T(8,128)S(1)}, f32[6,128,128]{2,1,0:T(8,128)S(1)}) custom-call(f32[6,128,128]{2,1,0:T(8,128)} %bitcast.10, f32[6,128,128]{2,1,0:T(8,128)} %bitcast.11, f32[6,128,128]{2,1,0:T(8,128)} %bitcast.12, f32[6,128,128]{2,1,0:T(8,128)} %bitcast.13, f32[128,128]{1,0:T(8,128)} %bitcast.14, f32[128,128]{1,0:T(8,128)} %bitcast.15, ...), custom_call_target="tpu_custom_call" | custom-call | tf_op jit(solution)/shard_map/pallas_call | solution.py:550
  20.1 0.9 %shard_map.123 = (f32[6,128,128]{2,1,0:T(8,128)}, f32[6,128,128]{2,1,0:T(8,128)}) custom-call(f32[6,128,128]{2,1,0:T(8,128)S(1)} %get-tuple-element.6.refs_0_, f32[6,128,128]{2,1,0:T(8,128)S(1)} %get-tuple-element.7.refs_1_), custom_call_target="tpu_custom_call" | custom-call | tf_op jit(solution)/shard_map/pallas_call | solution.py:560

commit v5 on v4

--- a/solution.py
+++ b/solution.py
@@ -435,6 +435,10 @@
     pack_span(ROTOR, 0)
     pl.semaphore_wait(barrier, npass + nspan - 2)
     start_far(ROTOR, 0)
+    for o in range(1, npass):
+        pl.semaphore_signal(
+            gate, inc=1, device_id=(lax.rem(ip + o, npass), js), device_id_type=MESH
+        )
     for c in loads[1:3]:
         c.wait()
     start_far(STATOR, 0)
@@ -443,15 +447,9 @@
     start_near(STATOR, 0)
     pack_span(STATOR, 0)
     start_span(STATOR, 0)
-    for o in range(1, npass):
-        pl.semaphore_signal(
-            gate, inc=1, device_id=(lax.rem(ip + o, npass), js), device_id_type=MESH
-        )
     for c in loads[3:7]:
         c.wait()
     pack_face(0, face_sums(0, range(1, cp - 1)))
-    pl.semaphore_wait(gate, npass - 1)
-    start_face(0)
 
     for r in range(2):
         clear(r)
@@ -462,6 +460,8 @@
     coef[STATOR][...] = RELAX / psi[STATOR][0][fields]
     interior(ROTOR, 0)
     interior(STATOR, 0)
+    pl.semaphore_wait(gate, npass - 1)
+    start_face(0)
 
     add_halos(ROTOR, 0, True)
     add_halos(STATOR, 0, True)

time: 21.2 us -> 21.2 us (level)
  no operation moved by 1% of the time
where the time goes in v5:
time: 21.2 us; the launch traced here: 21 us
  Pallas kernels  19.7 us (93%)
  between operations  1.29 us (6%)
    pallas_call x1, Pallas kernels, per_device(): pl.pallas_call(functools.partial(kernel, fields, cp, cs, ca, npass, nspan...  18.8 us
    pallas_call x1, Pallas kernels, per_device(): pl.pallas_call(write_out, out_shape=[pltpu.HBM(shape, F32)] * 2, in_specs...  0.89 us

profile of v5, /device:TPU:0, one launch (start us, length us, event | category | flops | bytes accessed | tf_op | source)
XLA Modules:
  0.0 21.0 jit_solution(867029338719042913)
XLA Ops:
  1.3 18.8 %shard_map.122 = (f32[6,128,128]{2,1,0:T(8,128)S(1)}, f32[6,128,128]{2,1,0:T(8,128)S(1)}) custom-call(f32[6,128,128]{2,1,0:T(8,128)} %bitcast.10, f32[6,128,128]{2,1,0:T(8,128)} %bitcast.11, f32[6,128,128]{2,1,0:T(8,128)} %bitcast.12, f32[6,128,128]{2,1,0:T(8,128)} %bitcast.13, f32[128,128]{1,0:T(8,128)} %bitcast.14, f32[128,128]{1,0:T(8,128)} %bitcast.15, ...), custom_call_target="tpu_custom_call" | custom-call | tf_op jit(solution)/shard_map/pallas_call | solution.py:550
  20.1 0.9 %shard_map.123 = (f32[6,128,128]{2,1,0:T(8,128)}, f32[6,128,128]{2,1,0:T(8,128)}) custom-call(f32[6,128,128]{2,1,0:T(8,128)S(1)} %get-tuple-element.6.refs_0_, f32[6,128,128]{2,1,0:T(8,128)S(1)} %get-tuple-element.7.refs_1_), custom_call_target="tpu_custom_call" | custom-call | tf_op jit(solution)/shard_map/pallas_call | solution.py:560

commit v6 on v5

--- a/solution.py
+++ b/solution.py
@@ -475,12 +475,15 @@
     interior(ROTOR, 2)
     interior(STATOR, 2)
 
-    for k in range(ITERS):
+    for k in range(ITERS - 1):
         for r in range(2):
             finish_sends(r, k)
         sent_faces(k).wait()
     add_halos(ROTOR, 2, False)
+    finish_sends(ROTOR, 2)
+    sent_faces(2).wait()
     add_inlet(2, False)
+    finish_sends(STATOR, 2)
     add_halos(STATOR, 2, False)
 
 

time: 21.2 us -> 21.2 us (level)
  no operation moved by 1% of the time
where the time goes in v6:
time: 21.2 us; the launch traced here: 21 us
  Pallas kernels  19.7 us (93%)
  between operations  1.29 us (6%)
    pallas_call x1, Pallas kernels, per_device(): pl.pallas_call(functools.partial(kernel, fields, cp, cs, ca, npass, nspan...  18.8 us
    pallas_call x1, Pallas kernels, per_device(): pl.pallas_call(write_out, out_shape=[pltpu.HBM(shape, F32)] * 2, in_specs...  0.89 us

profile of v6, /device:TPU:0, one launch (start us, length us, event | category | flops | bytes accessed | tf_op | source)
XLA Modules:
  0.0 21.0 jit_solution(12960576559763388147)
XLA Ops:
  1.3 18.8 %shard_map.122 = (f32[6,128,128]{2,1,0:T(8,128)S(1)}, f32[6,128,128]{2,1,0:T(8,128)S(1)}) custom-call(f32[6,128,128]{2,1,0:T(8,128)} %bitcast.10, f32[6,128,128]{2,1,0:T(8,128)} %bitcast.11, f32[6,128,128]{2,1,0:T(8,128)} %bitcast.12, f32[6,128,128]{2,1,0:T(8,128)} %bitcast.13, f32[128,128]{1,0:T(8,128)} %bitcast.14, f32[128,128]{1,0:T(8,128)} %bitcast.15, ...), custom_call_target="tpu_custom_call" | custom-call | tf_op jit(solution)/shard_map/pallas_call | solution.py:553
  20.1 0.9 %shard_map.123 = (f32[6,128,128]{2,1,0:T(8,128)}, f32[6,128,128]{2,1,0:T(8,128)}) custom-call(f32[6,128,128]{2,1,0:T(8,128)S(1)} %get-tuple-element.6.refs_0_, f32[6,128,128]{2,1,0:T(8,128)S(1)} %get-tuple-element.7.refs_1_), custom_call_target="tpu_custom_call" | custom-call | tf_op jit(solution)/shard_map/pallas_call | solution.py:563
